TPU v7x, 32 devices: a whole 2x2x4 slice. The times are simulated.
32 devices in a mesh: dp: 8 (over z, y), row: 2 (over core), col: 2 (over x).
Axes of the slice: x: 2, y: 2, z: 4, core: 2. Of those that a mesh axis runs over, the one named last changes fastest.
Arguments:
- tokens: bfloat16 [8192, 1024], P('dp', ('row', 'col')), may hold values from -6 to 6
- cotangent: bfloat16 [8192, 1024], P('dp', ('row', 'col')), may hold values from -6 to 6
- lengths: int32 [8, 4], P('dp'), may hold values from 1 to 800, 1024 in all within a row
- norm_gain: float32 [1024], replicated, may hold values from 0.5 to 1.5
- w_query: bfloat16 [1024, 1024], P(None, ('row', 'col')), may hold values from -0.1875 to 0.1875
- w_key: bfloat16 [1024, 1024], P(None, ('row', 'col')), may hold values from -0.1875 to 0.1875
- w_value: bfloat16 [1024, 2048], P(None, ('row', 'col')), may hold values from -0.1875 to 0.1875
- w_alpha: bfloat16 [1024, 8], P(None, ('row', 'col')), may hold values from -0.1875 to 0.1875
- w_beta: bfloat16 [1024, 8], P(None, ('row', 'col')), may hold values from -0.1875 to 0.1875
- conv_query: float32 [4, 1024], P(None, ('row', 'col')), may hold values from 0.2 to 1
- conv_key: float32 [4, 1024], P(None, ('row', 'col')), may hold values from 0.2 to 1
- conv_value: float32 [4, 2048], P(None, ('row', 'col')), may hold values from 0.2 to 1
- decay_log: float32 [8], P(('row', 'col')), may hold values from -6 to -1
- decay_bias: float32 [8], P(('row', 'col')), may hold values from -1.5 to 1
- w_outgate: bfloat16 [1024, 2048], P(None, ('row', 'col')), may hold values from -0.1875 to 0.1875
- out_gain: float32 [256], replicated, may hold values from 0.5 to 1.5
- w_out: bfloat16 [2048, 1024], P(('row', 'col')), may hold values from -0.125 to 0.125
- ffn_gain: float32 [1024], replicated, may hold values from 0.5 to 1.5
- w_gate: bfloat16 [1024, 2816], P(None, ('row', 'col')), may hold values from -0.1875 to 0.1875
- w_up: bfloat16 [1024, 2816], P(None, ('row', 'col')), may hold values from -0.1875 to 0.1875
- w_down: bfloat16 [2816, 1024], P(('row', 'col')), may hold values from -0.109375 to 0.109375
Outputs:
- output: bfloat16 [8192, 1024], P('dp', ('row', 'col'))
- input_grad: bfloat16 [8192, 1024], P('dp', ('row', 'col'))
- norm_gain_grad: float32 [1024], replicated
- w_query_grad: float32 [1024, 1024], P(None, ('row', 'col'))
- w_key_grad: float32 [1024, 1024], P(None, ('row', 'col'))
- w_value_grad: float32 [1024, 2048], P(None, ('row', 'col'))
- w_alpha_grad: float32 [1024, 8], P(None, ('row', 'col'))
- w_beta_grad: float32 [1024, 8], P(None, ('row', 'col'))
- conv_query_grad: float32 [4, 1024], P(None, ('row', 'col'))
- conv_key_grad: float32 [4, 1024], P(None, ('row', 'col'))
- conv_value_grad: float32 [4, 2048], P(None, ('row', 'col'))
- decay_log_grad: float32 [8], P(('row', 'col'))
- decay_bias_grad: float32 [8], P(('row', 'col'))
- w_outgate_grad: float32 [1024, 2048], P(None, ('row', 'col'))
- out_gain_grad: float32 [256], replicated
- w_out_grad: float32 [2048, 1024], P(('row', 'col'))
- ffn_gain_grad: float32 [1024], replicated
- w_gate_grad: float32 [1024, 2816], P(None, ('row', 'col'))
- w_up_grad: float32 [1024, 2816], P(None, ('row', 'col'))
- w_down_grad: float32 [2816, 1024], P(('row', 'col'))
Inputs may be any that keep to these rules, and one draw needn't show every extreme that they name: Each row holds the lengths of 4 documents that together fill one sequence of 1024 tokens; the longest of each row is exactly 800.
All inputs are finite; a program needn't handle non-finite values.
Results may differ from a plain program's by a relative error of at most 0.017.
Values may be sent and summed in bfloat16 or wider, within the bound.
No kernel may reach another device: no remote copies, remote signals or barrier semaphores. Data moves between devices by JAX's collectives and lax.ppermute only.
A program may use at most 192 MiB of HBM per device.

v0:
```python
import functools

import jax
import jax.numpy as jnp
from jax import lax
from jax.sharding import PartitionSpec as P

KH = 128
VH = 256
CONV = 4
SPAN = 64
SEQ_LEN = 1024


epsilon = 1e-06
out_epsilon = 0.05
highest = lax.Precision.HIGHEST


def rms_scale(values, scales):
    return values * lax.rsqrt(jnp.mean(values * values, axis=-1, keepdims=True) + epsilon) * scales


def head_scale(values, scales):
    return (
        values * lax.rsqrt(jnp.mean(values * values, axis=-1, keepdims=True) + out_epsilon) * scales
    )


def segments_of(lengths):
    doc_ends = jnp.cumsum(lengths, axis=-1, dtype=jnp.int32)
    places = jnp.arange(SEQ_LEN, dtype=jnp.int32)
    counted = (places[None, :, None] >= doc_ends[:, None, :]).astype(jnp.int32)
    return jnp.sum(counted, axis=-1, dtype=jnp.int32)


def short_conv(values, kernel, segment):
    summed = values * kernel[CONV - 1]
    for offset in range(1, CONV):
        shifted = jnp.pad(values[:, :-offset], ((0, 0), (offset, 0), (0, 0)))
        before = jnp.pad(segment[:, :-offset], ((0, 0), (offset, 0)), constant_values=-1)
        linked = (before == segment).astype(jnp.float32)
        summed = summed + shifted * linked[..., None] * kernel[CONV - 1 - offset]
    return jax.nn.silu(summed)


def to_blocks(values, seq_count, block_count, head_count):
    return jnp.moveaxis(values.reshape(seq_count, block_count, SPAN, head_count, -1), 3, 1)


def delta_rule(queries, key_heads, values, beta_rate, decay_rate, segment):
    seq_count, length, head_count = (queries.shape[0], queries.shape[1], queries.shape[2])
    block_count = length // SPAN
    query_b = to_blocks(queries, seq_count, block_count, head_count)
    key_b = to_blocks(key_heads, seq_count, block_count, head_count)
    value_b = to_blocks(values, seq_count, block_count, head_count)
    beta_b = to_blocks(beta_rate[..., None], seq_count, block_count, head_count)[..., 0]
    cumulative = jnp.cumsum(
        to_blocks(decay_rate[..., None], seq_count, block_count, head_count)[..., 0], axis=-1
    )
    seg_b = segment.reshape(seq_count, block_count, SPAN)
    before = jnp.concatenate([jnp.full((seq_count, 1), -1, jnp.int32), seg_b[:, :-1, -1]], axis=1)
    carried = (seg_b == before[..., None]).astype(jnp.float32)[:, None]
    positions = jnp.arange(SPAN, dtype=jnp.int32)
    below_mask = positions[:, None] >= positions[None, :]
    strict = (positions[:, None] > positions[None, :]).astype(jnp.float32)
    linked = ((seg_b[..., :, None] == seg_b[..., None, :]) & below_mask)[:, None]
    spread = cumulative[..., :, None] - cumulative[..., None, :]
    within = jnp.where(linked, jnp.exp(jnp.where(linked, spread, 0.0)), 0.0)
    key_gram = jnp.einsum("shncd,shnmd->shncm", key_b, key_b, precision=highest)
    system = jnp.eye(SPAN, dtype=jnp.float32) + beta_b[..., None] * within * strict * key_gram
    initial = jnp.exp(cumulative) * carried
    pseudo = lax.linalg.triangular_solve(
        system, beta_b[..., None] * value_b, left_side=True, lower=True, unit_diagonal=True
    )
    correct = lax.linalg.triangular_solve(
        system,
        (beta_b * initial)[..., None] * key_b,
        left_side=True,
        lower=True,
        unit_diagonal=True,
    )
    scores = jnp.einsum("shncd,shnmd->shncm", query_b, key_b, precision=highest) * within
    tail_mask = (seg_b == seg_b[..., -1:]).astype(jnp.float32)[:, None]
    tail_decay = jnp.exp(cumulative[..., -1:] - cumulative) * tail_mask
    end_decay = jnp.exp(cumulative[..., -1]) * carried[..., -1]

    def advance(memory, pieces):
        pseudo_c, correct_c, query_c, key_c, scores_c, initial_c, tail_c, end_c = pieces
        delta_value = pseudo_c - jnp.einsum("shck,shvk->shcv", correct_c, memory, precision=highest)
        result = jnp.einsum(
            "shck,shvk->shcv", initial_c[..., None] * query_c, memory, precision=highest
        )
        result = result + jnp.einsum("shcm,shmv->shcv", scores_c, delta_value, precision=highest)
        memory = end_c[..., None, None] * memory + jnp.einsum(
            "shcv,shck->shvk", tail_c[..., None] * delta_value, key_c, precision=highest
        )
        return (memory, result)

    def leading(array):
        return jnp.moveaxis(array, 2, 0)

    memory = jnp.zeros((seq_count, head_count, values.shape[-1], queries.shape[-1]), jnp.float32)
    pieces = tuple(
        (
            leading(item)
            for item in (pseudo, correct, query_b, key_b, scores, initial, tail_decay, end_decay)
        )
    )
    memory, results = lax.scan(advance, memory, pieces)
    results = jnp.moveaxis(jnp.moveaxis(results, 0, 2), 1, 3)
    return results.reshape(seq_count, length, head_count, -1)


def mixer_core(
    query_proj,
    key_proj,
    value_proj,
    alpha_proj,
    beta_proj,
    gate_proj,
    conv_query,
    conv_key,
    conv_value,
    decay_log,
    decay_bias,
    out_gain,
    segment,
):
    seq_count, length = segment.shape
    head_count = alpha_proj.shape[-1]
    queries = short_conv(query_proj, conv_query, segment).reshape(seq_count, length, head_count, KH)
    key_heads = short_conv(key_proj, conv_key, segment).reshape(seq_count, length, head_count, KH)
    key_heads = key_heads * lax.rsqrt(
        jnp.sum(key_heads * key_heads, axis=-1, keepdims=True) + epsilon
    )
    values = short_conv(value_proj, conv_value, segment).reshape(seq_count, length, head_count, VH)
    beta_rate = jax.nn.sigmoid(beta_proj)
    decay_rate = -jnp.exp(decay_log) * jax.nn.softplus(alpha_proj + decay_bias)
    result = delta_rule(queries, key_heads, values, beta_rate, decay_rate, segment)
    gate_act = jax.nn.silu(gate_proj.reshape(seq_count, length, head_count, VH))
    normed = head_scale(result, out_gain) * gate_act
    return normed.reshape(seq_count, length, head_count * VH)


def plain_product(first_mat, second_mat):
    return jnp.dot(first_mat, second_mat, preferred_element_type=jnp.float32)


def left_product(first_mat, second_mat):
    return lax.dot_general(
        first_mat, second_mat, (((0,), (0,)), ((), ())), preferred_element_type=jnp.float32
    )


def right_product(first_mat, second_mat):
    return lax.dot_general(
        first_mat, second_mat, (((1,), (1,)), ((), ())), preferred_element_type=jnp.float32
    )


def norm_back(inputs, scales, grad_normed):
    inverse = lax.rsqrt(jnp.mean(inputs * inputs, axis=-1, keepdims=True) + epsilon)
    weighted = scales * grad_normed
    grad_inputs = inverse * weighted - inputs * (inverse * inverse * inverse) * jnp.mean(
        weighted * inputs, axis=-1, keepdims=True
    )
    grad_scales = jnp.sum(grad_normed * inputs * inverse, axis=0)
    return (grad_inputs, grad_scales)


def body(
    tokens,
    cotangent,
    lengths,
    norm_gain,
    w_query,
    w_key,
    w_value,
    w_alpha,
    w_beta,
    conv_query,
    conv_key,
    conv_value,
    decay_log,
    decay_bias,
    w_outgate,
    out_gain,
    w_out,
    ffn_gain,
    w_gate,
    w_up,
    w_down,
):
    seq_count = lengths.shape[0]
    width_part = tokens.shape[1]
    place = lax.axis_index(("row", "col"))
    segment = segments_of(lengths)
    whole = lax.all_gather(tokens, ("row", "col"), axis=1, tiled=True).astype(jnp.float32)
    normed = rms_scale(whole, norm_gain).astype(jnp.bfloat16)
    proj_weights = (w_query, w_key, w_value, w_alpha, w_beta, w_outgate)
    projections = tuple(
        (plain_product(normed, weight).reshape(seq_count, SEQ_LEN, -1) for weight in proj_weights)
    )
    smaller = tuple(
        (item for item in (conv_query, conv_key, conv_value, decay_log, decay_bias, out_gain))
    )
    mixed, mixer_pull = jax.vjp(
        functools.partial(mixer_core, segment=segment), *projections + smaller
    )
    mixed_low = mixed.reshape(seq_count * SEQ_LEN, -1).astype(jnp.bfloat16)
    partial_out = plain_product(mixed_low, w_out)
    hidden_own = tokens.astype(jnp.float32) + lax.psum_scatter(
        partial_out, ("row", "col"), scatter_dimension=1, tiled=True
    )
    hidden = lax.all_gather(hidden_own, ("row", "col"), axis=1, tiled=True)
    normed_ffn = rms_scale(hidden, ffn_gain).astype(jnp.bfloat16)
    gate_act = plain_product(normed_ffn, w_gate)
    up_act = plain_product(normed_ffn, w_up)
    sigma = jax.nn.sigmoid(gate_act)
    product = (gate_act * sigma * up_act).astype(jnp.bfloat16)
    ffn_share = lax.psum_scatter(
        plain_product(product, w_down).astype(jnp.bfloat16),
        ("row", "col"),
        scatter_dimension=1,
        tiled=True,
    ).astype(jnp.float32)
    output = (hidden_own + ffn_share).astype(jnp.bfloat16)
    grad_out = lax.all_gather(cotangent, ("row", "col"), axis=1, tiled=True)
    grad_product = right_product(grad_out, w_down)
    grad_down = left_product(product, grad_out)
    grad_gate_act = (grad_product * up_act * sigma * (1.0 + gate_act * (1.0 - sigma))).astype(
        jnp.bfloat16
    )
    grad_up_act = (grad_product * gate_act * sigma).astype(jnp.bfloat16)
    grad_gate = left_product(normed_ffn, grad_gate_act)
    grad_up = left_product(normed_ffn, grad_up_act)
    grad_normed_ffn = right_product(grad_gate_act, w_gate) + right_product(grad_up_act, w_up)
    grad_hidden_part, grad_ffn_gain = norm_back(hidden, ffn_gain, grad_normed_ffn)
    ffn_sums = (grad_gate, grad_up, grad_down)
    own_grad = cotangent.astype(jnp.float32) + lax.psum_scatter(
        grad_hidden_part.astype(jnp.bfloat16), ("row", "col"), scatter_dimension=1, tiled=True
    ).astype(jnp.float32)
    grad_hidden = lax.all_gather(
        own_grad.astype(jnp.bfloat16), ("row", "col"), axis=1, tiled=True
    ).astype(own_grad.dtype)
    grad_hidden_low = grad_hidden.astype(jnp.bfloat16)
    grad_hidden_own = lax.dynamic_slice_in_dim(
        grad_hidden_low, place * width_part, width_part, 1
    ).astype(jnp.float32)
    grad_out_proj = left_product(mixed_low, grad_hidden_low)
    grad_mixed = right_product(grad_hidden_low, w_out).reshape(mixed.shape)
    pulled = mixer_pull(grad_mixed)
    proj_grads = tuple(
        (item.reshape(seq_count * SEQ_LEN, -1).astype(jnp.bfloat16) for item in pulled[:6])
    )
    weight_grads = tuple((left_product(normed, item) for item in proj_grads))
    grad_normed = right_product(proj_grads[0], w_query) + right_product(proj_grads[1], w_key)
    grad_normed = (
        grad_normed + right_product(proj_grads[2], w_value) + right_product(proj_grads[3], w_alpha)
    )
    grad_normed = (
        grad_normed + right_product(proj_grads[4], w_beta) + right_product(proj_grads[5], w_outgate)
    )
    grad_input_part, grad_norm_gain = norm_back(whole, norm_gain, grad_normed)
    input_grad = (
        grad_hidden_own
        + lax.psum_scatter(
            grad_input_part.astype(jnp.bfloat16), ("row", "col"), scatter_dimension=1, tiled=True
        ).astype(jnp.float32)
    ).astype(jnp.bfloat16)
    gains = lax.psum((grad_norm_gain, grad_ffn_gain, pulled[11]), ("dp", "row", "col"))
    summed = lax.psum(
        (
            weight_grads[0],
            weight_grads[1],
            weight_grads[2],
            weight_grads[3],
            weight_grads[4],
            pulled[6],
            pulled[7],
            pulled[8],
            pulled[9],
            pulled[10],
            weight_grads[5],
            grad_out_proj,
            ffn_sums[0],
            ffn_sums[1],
            ffn_sums[2],
        ),
        "dp",
    )
    mixer_sums = summed[:12]
    ffn_sums = summed[12:]
    return (
        output,
        input_grad,
        gains[0],
        mixer_sums[0],
        mixer_sums[1],
        mixer_sums[2],
        mixer_sums[3],
        mixer_sums[4],
        mixer_sums[5],
        mixer_sums[6],
        mixer_sums[7],
        mixer_sums[8],
        mixer_sums[9],
        mixer_sums[10],
        gains[2],
        mixer_sums[11],
        gains[1],
        ffn_sums[0],
        ffn_sums[1],
        ffn_sums[2],
    )


def solution(mesh):
    placed = (
        P("dp", ("row", "col")),
        P("dp", ("row", "col")),
        P("dp", None),
        P(),
        P(None, ("row", "col")),
        P(None, ("row", "col")),
        P(None, ("row", "col")),
        P(None, ("row", "col")),
        P(None, ("row", "col")),
        P(None, ("row", "col")),
        P(None, ("row", "col")),
        P(None, ("row", "col")),
        P(("row", "col")),
        P(("row", "col")),
        P(None, ("row", "col")),
        P(),
        P(("row", "col"), None),
        P(),
        P(None, ("row", "col")),
        P(None, ("row", "col")),
        P(("row", "col"), None),
    )
    return jax.shard_map(
        body,
        mesh=mesh,
        in_specs=placed,
        out_specs=(
            P("dp", ("row", "col")),
            P("dp", ("row", "col")),
            P(),
            P(None, ("row", "col")),
            P(None, ("row", "col")),
            P(None, ("row", "col")),
            P(None, ("row", "col")),
            P(None, ("row", "col")),
            P(None, ("row", "col")),
            P(None, ("row", "col")),
            P(None, ("row", "col")),
            P(("row", "col")),
            P(("row", "col")),
            P(None, ("row", "col")),
            P(),
            P(("row", "col"), None),
            P(),
            P(None, ("row", "col")),
            P(None, ("row", "col")),
            P(("row", "col"), None),
        ),
        check_vma=False,
    )
```

profile of v0, /device:TPU:0, one launch (start us, length us, event | category | flops | bytes accessed | tf_op | source)
XLA Modules:
  0.0 1862.2 jit_solution(609048775729841754)
XLA Ops:
  20.0 15.2 all-gather.5.cloned.1.call-done
  41.1 3.9 fusion.175
  51.9 4.7 fusion.161
  75.0 3.6 copy.353
  78.6 4.4 fusion.159
  91.8 159.0 %custom-call.12 = f32[1,2,16,1,64,64]{4,5,3,2,1,0:T(8,128)} custom-call(f32[1,2,16,1,64,64]{5,4,3,2,1,0:T(8,128)} %get-tuple-element.1090), custom_call_target="InvertDiagBlocksLowerTriangular" | custom-call | tf_op jit(solution)/shard_map/jvp()/triangular_solve | solution.py:73
  251.7 5.7 fusion.107
  269.6 233.7 %while.58 = (s32[]{:T(128)}, f32[1,2,256,128]{3,2,1,0:T(8,128)}, f32[16,1,2,64,256]{4,3,2,1,0:T(8,128)}, f32[16,1,2,256,128]{4,3,2,1,0:T(8,128)}, f32[16,1,2,64,...) while((s32[]{:T(128)}, f32[1,2,256,128]{3,2,1,0:T(8,128)}, ...), condition=%wide.region_6.7_spmd.clone, body=%wide.region_5.6_spmd.clone.sunk | while | flops 176717824 | bytes 3156741 | solution.py:110
  523.2 44.6 %reduce-scatter.5.cloned.1.call-done = f32[1024,256]{1,0:T(8,128)} async-done(((f32[1024,1024]{1,0:T(8,128)}), f32[1024,256]{1,0:T(8,128)}) %reduce-scatter.5.cloned.1.call-update) | async-done | bytes 1048592 | tf_op jit(solution)/shard_map/reduce_scatter | solution.py:213
  570.9 34.0 %all-gather.7.cloned.1.call-done = f32[1024,1024]{1,0:T(8,128)} async-done(((f32[1024,256]{1,0:T(8,128)}), f32[1024,1024]{1,0:T(8,128)}) %all-gather.7.cloned.1.call-update) | async-done | bytes 4194320 | tf_op jit(solution)/shard_map/all_gather | solution.py:216
  616.3 13.0 all-gather.9.cloned.1.call-done
  629.3 6.5 multiply_convert_fusion.1
  644.6 31.5 %reduce-scatter.9.cloned.1.call-done = bf16[1024,256]{1,0:T(8,128)(2,1)} async-done(((bf16[1024,1024]{1,0:T(8,128)(2,1)}), bf16[1024,256]{1,0:T(8,128)(2,1)}) %reduce-scatter.9.cloned.1.call-update) | async-done | bytes 524304 | tf_op jit(solution)/shard_map/reduce_scatter | solution.py:241
  697.1 158.7 %custom-call.16 = f32[1,2,16,1,64,64]{4,5,3,2,1,0:T(8,128)} custom-call(f32[1,2,16,1,64,64]{5,4,3,2,1,0:T(8,128)} %fusion.153), custom_call_target="InvertDiagBlocksLowerTriangular" | custom-call | tf_op jit(solution)/shard_map/transpose(jvp())/triangular_solve/custom-call.3 | solution.py:76
  855.8 4.6 convolution_convert_fusion
  861.6 7.0 fusion.102
  868.6 4.0 reshape_reshape.6
  872.6 3.8 multiply_reduce_fusion.3
  884.1 274.8 %while.59 = (s32[]{:T(128)}, f32[1,2,256,128]{3,2,1,0:T(8,128)S(1)}, f32[16,1,2,64,256]{4,3,2,1,0:T(8,128)}, f32[16,1,2,64,128]{4,3,2,1,0:T(8,128)}, f32[16,1,2,...) while((s32[]{:T(128)}, ...), condition=%wide.region_18.19_spmd.clone, body=%wide.region_14.18_spmd.clone.sunk | while | flops 353156864 | bytes 5063995 | solution.py:110
  1159.0 4.4 fusion.114
  1171.8 4.8 fusion.146
  1176.6 3.7 convolution_bitcast_fusion.8
  1186.2 3.9 reshape.1399
  1190.1 6.5 multiply_reduce_fusion.7
  1201.6 4.5 fusion.127
  1215.8 4.1 fusion.123
  1225.3 5.7 multiply_reduce_fusion.17
  1263.6 5.9 fusion.96
  1271.9 5.4 fusion.271
  1298.3 42.8 %all-reduce.35 = (f32[1024]{0:T(1024)}, f32[256]{0:T(256)}, f32[1024]{0:T(1024)}) all-reduce(f32[1024]{0:T(1024)S(1)} %get-tuple-element.937, f32[256]{0:T(256)S(1)} %get-tuple-element.939, f32[1024]{0:T(1024)S(1)} %copy-done.126), channel_id=1, replica_groups=mesh['dp'=8,'row'=2,'col'=2] {'dp','row','col'}, use_global_device_ids=true, to_apply=%region_30.32 | all-reduce | flops 2304 | bytes 18432 | tf_op jit(solution)/shard_map/psum | solution.py:272
  1342.0 41.5 %all-reduce.36 = (f32[1024,2]{0,1:T(2,128)}, f32[1024,2]{0,1:T(2,128)}, f32[4,256]{1,0:T(4,128)}, f32[4,256]{1,0:T(4,128)}, f32[4,512]{1,0:T(4,128)}, /*index=5*/f32[2]{0:T(128)}, f32[2]{0:T(128)}) all-reduce(f32[1024,2]{0,1:T(2,128)S(1)} %fusion.228, f32[1024,2]{0,1:T(2,128)S(1)} %fusion.250, ...), channel_id=1, replica_groups=mesh['dp'=8,'row'=2,'col'=2] {'dp'}, use_global_device_ids=true, to_apply=%region_34.36 | all-reduce | flops 8196 | bytes 65568 | tf_op jit(solution)/shard_map/psum | solution.py:273
  1385.6 452.0 %all-reduce.40.cloned.1.call-done = (f32[1024,256]{1,0:T(8,128)}, f32[1024,256]{1,0:T(8,128)}, f32[1024,512]{1,0:T(8,128)}, f32[1024,512]{1,0:T(8,128)}, f32[512...) async-done(((f32[1024,256]{1,0:T(8,128)}, f32[1024,256]{1,0:T(8,128)}, f32[1024,512]{1,0:T(8,128)}, f32[1024,512]{1,0:T(8,128)}, ...) | async-done | bytes 17039376 | tf_op jit(solution)/shard_map/psum | solution.py:273
  (932 shorter events, 756.4 us)
Async XLA Ops:
  7.2 622.1 %copy-start = (bf16[704,1024]{1,0:T(8,128)(2,1)S(1)}, bf16[704,1024]{1,0:T(8,128)(2,1)}, u32[]{:S(2)}) copy-start(bf16[704,1024]{1,0:T(8,128)(2,1)} %param.47) | copy-start | bytes 4325380
  7.2 30.8 %copy-start.110 = (f32[1024]{0:T(1024)S(1)}, f32[1024]{0:T(1024)}, u32[]{:S(2)}) copy-start(f32[1024]{0:T(1024)} %param.30) | copy-start | bytes 12292
  7.2 28.0 %all-gather.5.cloned.1.call-start = ((), (), s32[]{:S(2)}) async-start(), calls=%async_computation.4 | async-start | bytes 2621440 | tf_op jit(solution)/shard_map/all_gather | solution.py:199
  8.0 559.8 %reduce-scatter.5.cloned.1.call-start = ((), (), s32[]{:S(2)}) async-start(), calls=%async_computation.5 | async-start | bytes 5242880 | tf_op jit(solution)/shard_map/reduce_scatter | solution.py:213
  17.8 23.2 %copy-start.85 = (f32[1,1024]{1,0:T(1,128)}, f32[1,1024]{1,0:T(1,128)S(1)}, u32[]{:S(2)}) copy-start(f32[1,1024]{1,0:T(1,128)S(1)} %get-tuple-element.1120) | copy-start | bytes 12292
  17.8 23.2 %copy-start.88 = (f32[1,1024]{1,0:T(1,128)}, f32[1,1024]{1,0:T(1,128)S(1)}, u32[]{:S(2)}) copy-start(f32[1,1024]{1,0:T(1,128)S(1)} %get-tuple-element.1121) | copy-start | bytes 12292
  17.8 23.2 %copy-start.91 = (f32[1,1024]{1,0:T(1,128)}, f32[1,1024]{1,0:T(1,128)S(1)}, u32[]{:S(2)}) copy-start(f32[1,1024]{1,0:T(1,128)S(1)} %get-tuple-element.1122) | copy-start | bytes 12292
  51.9 6.1 copy-start.66
  51.9 6.1 copy-start.127
  51.9 6.1 copy-start.151
  51.9 6.0 copy-start.153
  251.6 5.7 copy-start.80
  251.6 5.7 copy-start.5
  251.6 5.7 copy-start.26
  251.6 5.7 copy-start.67
  523.1 81.8 %all-gather.7.cloned.1.call-start = ((), (), s32[]{:S(2)}) async-start(), calls=%async_computation.6 | async-start | bytes 5242880 | tf_op jit(solution)/shard_map/all_gather | solution.py:216
  570.2 59.0 %all-gather.9.cloned.1.call-start = ((), (), s32[]{:S(2)}) async-start(), calls=%async_computation.8 | async-start | bytes 2621440 | tf_op jit(solution)/shard_map/all_gather | solution.py:229
  570.8 105.3 %reduce-scatter.9.cloned.1.call-start = ((), (), s32[]{:S(2)}) async-start(), calls=%async_computation.9 | async-start | bytes 2621440 | tf_op jit(solution)/shard_map/reduce_scatter | solution.py:241
  629.3 6.5 copy-start.156
  644.6 215.9 %all-gather.11.cloned.1.call-start = ((), (), s32[]{:S(2)}) async-start(), calls=%async_computation.10 | async-start | bytes 2621440 | tf_op jit(solution)/shard_map/all_gather | solution.py:244
  678.3 616.9 %reduce-scatter.7.cloned.1.call-start = ((), (), s32[]{:S(2)}) async-start(), calls=%async_computation.7 | async-start | bytes 2621440 | tf_op jit(solution)/shard_map/reduce_scatter | solution.py:222
  860.4 523.1 %reduce-scatter.11.cloned.1.call-start = ((), (), s32[]{:S(2)}) async-start(), calls=%async_computation.11 | async-start | bytes 2621440 | tf_op jit(solution)/shard_map/reduce_scatter | solution.py:268
  1190.1 6.5 copy-start.109
  1190.1 6.5 copy-start.120
  1225.3 5.7 copy-start.142
  1225.3 5.7 copy-start.144
  1231.0 5.8 copy-start.19
  1231.0 5.8 copy-start.21
  1250.9 7.9 copy-start.37
  1263.6 5.9 copy-start.123
  1271.8 565.7 %all-reduce.40.cloned.1.call-start = ((), (), s32[]{:S(2)}) async-start(), calls=%async_computation.12 | async-start | bytes 34078720 | tf_op jit(solution)/shard_map/psum | solution.py:273
  1295.2 46.0 %copy-start.160 = (f32[2]{0:T(128)S(1)}, f32[2]{0:T(128)}, u32[]{:S(2)}) copy-start(f32[2]{0:T(128)} %param.39) | copy-start | bytes 28
  (140 other events, 372.0 us)
Sparse Core Ops, SparseCore 0:
  9.6 25.5 all-gather.4
  523.3 44.4 reduce-scatter.4
  570.4 34.4 all-gather.6
  606.4 22.8 all-gather.8
  644.7 31.4 reduce-scatter.8
  678.4 22.8 all-gather.10
  860.5 31.5 reduce-scatter.6
  1272.0 31.6 reduce-scatter.10
  1311.2 526.2 all-reduce.39
where the time goes:
time: 1880 us; the launch traced here: 1860 us
  waiting for transfers between devices  592 us (31%)
  other arithmetic  492 us (26%)
  matrix products  472 us (25%)
  local copies, waits for them, and re-layouts  206 us (11%)
  blocking collectives  84.3 us (4%)
    psum x1, waiting for transfers between devices, body(): lax.psum((weight_grads[0], weight_grads[1], weight_grads[2], weight_grads...  452 us
    another operation x2, other arithmetic, delta_rule(): lax.linalg.triangular_solve(system, (beta_b * initial)[..., None] * key_b...  161 us
    another operation x3, other arithmetic, delta_rule(): lax.linalg.triangular_solve(system, beta_b[..., None] * value_b, left_sid...  160 us
    dot_general x48, matrix products, advance(): jnp.einsum('shcv,shck->shvk', tail_c[..., None] * delta_value, key_c, pre...  89.2 us
    dot_general x48, matrix products, advance(): jnp.einsum('shcm,shmv->shcv', scores_c, delta_value, precision=highest)  87.8 us
    dot_general x48, matrix products, advance(): jnp.einsum('shck,shvk->shcv', correct_c, memory, precision=highest)  86.6 us
    dot_general x48, matrix products, advance(): jnp.einsum('shck,shvk->shcv', initial_c[..., None] * query_c, memory, pre...  77.8 us
    dynamic_update_slice x32, other arithmetic, delta_rule(): memory, results = lax.scan(advance, memory, pieces)  50.7 us
  transfers between devices with their start and end apart: 9, of which 6 were waited for; matrix products, arithmetic and copies ran while one was open for 34% of the time, Pallas kernels for 0%

commit v1 on v0

v1 whole, which is shorter than its diff:
```python
import functools

import jax
import jax.numpy as jnp
from jax import lax
from jax.experimental import pallas as pl
from jax.experimental.pallas import tpu as pltpu
from jax.sharding import PartitionSpec as P

KH = 128
VH = 256
CONV = 4
BLOCK = 128
TAIL = 128

epsilon = 1e-06
out_epsilon = 0.05

NN = (((1,), (0,)), ((), ()))
NT = (((1,), (1,)), ((), ()))
TN = (((0,), (0,)), ((), ()))


def product_one(first, second, dims=NN):
    return lax.dot_general(
        first.astype(jnp.bfloat16),
        second.astype(jnp.bfloat16),
        dims,
        preferred_element_type=jnp.float32,
    )


def product_three(first, second, dims=NN):
    first_high = first.astype(jnp.bfloat16)
    second_high = second.astype(jnp.bfloat16)
    first_low = (first - first_high.astype(jnp.float32)).astype(jnp.bfloat16)
    second_low = (second - second_high.astype(jnp.float32)).astype(jnp.bfloat16)
    dot = functools.partial(
        lax.dot_general, dimension_numbers=dims, preferred_element_type=jnp.float32
    )
    return dot(first_high, second_high) + (
        dot(first_high, second_low) + dot(first_low, second_high)
    )


def product_six(first, second, dims=NN):
    return lax.dot_general(
        first, second, dims, precision=lax.Precision.HIGHEST, preferred_element_type=jnp.float32
    )


mm_sum = product_six
mm_inverse = product_three
mm_chain = product_three
mm_gram = product_three
mm_out = product_three
mm_back = product_three


def sigmoid(values):
    return 1.0 / (1.0 + jnp.exp(-values))


def softplus(values):
    return jnp.maximum(values, 0.0) + jnp.log1p(jnp.exp(-jnp.abs(values)))


def document_starts(lengths_ref, positions):
    starts = jnp.zeros_like(positions)
    end = 0
    for doc in range(lengths_ref.shape[1] - 1):
        end = end + lengths_ref[0, doc]
        starts = jnp.where(positions >= end, end, starts)
    return starts


def start_of(lengths_ref, position):
    start = 0
    end = 0
    for doc in range(lengths_ref.shape[1] - 1):
        end = end + lengths_ref[0, doc]
        start = jnp.where(position >= end, end, start)
    return start


def unit_inverses(lowers):
    size = lowers[0].shape[0]
    row = lax.broadcasted_iota(jnp.int32, (size, size), 0)
    column = lax.broadcasted_iota(jnp.int32, (size, size), 1)
    eye = (row == column).astype(jnp.float32)
    within = (row >> 3) == (column >> 3)
    inner = [jnp.where(within, low, 0.0) for low in lowers]
    square = [mm_inverse(one, one) for one in inner]
    cube = [mm_inverse(one, two) for one, two in zip(inner, square)]
    fourth = [mm_inverse(two, two) for two in square]
    part = [eye - one + two - three for one, two, three in zip(inner, square, cube)]
    result = [one + mm_inverse(one, four) for one, four in zip(part, fourth)]
    shift = 3
    while (1 << shift) < size:
        off = ((row >> (shift + 1)) == (column >> (shift + 1))) & (
            (row >> shift) != (column >> shift)
        )
        edge = [mm_inverse(jnp.where(off, low, 0.0), one) for low, one in zip(lowers, result)]
        result = [one - mm_inverse(one, two) for one, two in zip(result, edge)]
        shift += 1
    return result


def window_before(ref, start, columns):
    early = pl.multiple_of(jnp.maximum(start - 8, 0), 8)
    return jnp.concatenate(
        [ref[pl.ds(early, 8), columns], ref[pl.ds(start, BLOCK), columns]], axis=0
    )


def decays(tail, scales, biases):
    logits = tail + biases
    return -jnp.exp(scales) * softplus(logits), logits


def block_masks(lengths_ref, start):
    positions = start + lax.broadcasted_iota(jnp.int32, (BLOCK, 1), 0)
    starts = document_starts(lengths_ref, positions)
    columns = start + lax.broadcasted_iota(jnp.int32, (BLOCK, BLOCK), 1)
    rows = start + lax.broadcasted_iota(jnp.int32, (BLOCK, BLOCK), 0)
    linked = (starts <= columns) & (rows >= columns)
    strict = rows > columns
    carried = (starts < start).astype(jnp.float32)
    last_start = start_of(lengths_ref, start + BLOCK - 1)
    tail_mask = (positions >= last_start).astype(jnp.float32)
    last_carried = (last_start < start).astype(jnp.float32)
    return positions - starts, linked, strict, carried, tail_mask, last_carried


def lower_ones():
    row = lax.broadcasted_iota(jnp.int32, (BLOCK, BLOCK), 0)
    column = lax.broadcasted_iota(jnp.int32, (BLOCK, BLOCK), 1)
    return (row >= column).astype(jnp.float32)


def head_decay(cumulative, flipped, head, linked, carried, tail_mask, last_carried):
    cum = cumulative[:, head : head + 1]
    spread = cum - flipped[head : head + 1, :]
    within = jnp.where(linked, jnp.exp(jnp.where(linked, spread, 0.0)), 0.0)
    last = cumulative[BLOCK - 1 : BLOCK, head : head + 1]
    initial = jnp.exp(cum) * carried
    tail = jnp.exp(last - cum) * tail_mask
    end = jnp.exp(last) * last_carried
    return within, initial, tail, end


def forward_kernel(
    heads,
    lengths_ref,
    proj_ref,
    filter_ref,
    decay_ref,
    gain_ref,
    mixed_ref,
    act_ref,
    inverse_ref,
    state_ref,
    delta_ref,
    result_ref,
    score_ref,
    gram_ref,
    query_ref,
    step_ref,
    pseudo_ref,
    correct_ref,
    add_ref,
):
    length = proj_ref.shape[0]
    blocks = length // BLOCK
    key_dim, value_dim = heads * KH, heads * VH
    tail_at = 2 * key_dim + 2 * value_dim
    widths = ((0, key_dim), (key_dim, 2 * key_dim), (2 * key_dim, 2 * key_dim + value_dim))

    def first(block, _):
        start = pl.multiple_of(block * BLOCK, BLOCK)
        rows = pl.ds(start, BLOCK)
        since, linked, strict, carried, tail_mask, last_carried = block_masks(lengths_ref, start)
        for low, high in widths:
            columns = slice(low, high)
            seen = window_before(proj_ref, start, columns)
            summed = seen[8:] * filter_ref[CONV - 1 : CONV, columns]
            for offset in range(1, CONV):
                tap = CONV - 1 - offset
                mask = (since >= offset).astype(jnp.float32)
                summed = summed + seen[8 - offset : 8 - offset + BLOCK] * (
                    mask * filter_ref[tap : tap + 1, columns]
                )
            act_ref[rows, columns] = summed
        tail_tile = proj_ref[rows, tail_at : tail_at + TAIL]
        rate, _ = decays(tail_tile, decay_ref[0:1, :], decay_ref[1:2, :])
        beta_tile = sigmoid(tail_tile)
        cumulative = mm_sum(lower_ones(), rate)
        flipped = cumulative.T
        lowers, kept = [], []
        for head in range(heads):
            key_cols = slice(head * KH, (head + 1) * KH)
            within, initial, tail, end = head_decay(
                cumulative, flipped, head, linked, carried, tail_mask, last_carried
            )
            beta = beta_tile[:, heads + head : heads + head + 1]
            summed = act_ref[rows, key_cols]
            query = summed * sigmoid(summed)
            summed = act_ref[rows, key_dim + head * KH : key_dim + (head + 1) * KH]
            key = summed * sigmoid(summed)
            key = key * lax.rsqrt(jnp.sum(key * key, axis=-1, keepdims=True) + epsilon)
            summed = act_ref[rows, 2 * key_dim + head * VH : 2 * key_dim + (head + 1) * VH]
            value = summed * sigmoid(summed)
            both = mm_gram(jnp.concatenate([key, query], axis=0), key, NT)
            gram = both[:BLOCK] * jnp.where(strict, within, 0.0)
            score = both[BLOCK:] * within
            lowers.append(beta * gram)
            kept.append((query * initial, key, value, beta, initial, tail, end, score))
            at = pl.ds(pl.multiple_of((block * heads + head) * BLOCK, BLOCK), BLOCK)
            gram_ref[at, :] = gram
            score_ref[at, :] = score
        inverses = unit_inverses(lowers)
        row = lax.broadcasted_iota(jnp.int32, (KH, KH), 0)
        column = lax.broadcasted_iota(jnp.int32, (KH, KH), 1)
        for head in range(heads):
            query, key, value, beta, initial, tail, end, score = kept[head]
            at = pl.ds(pl.multiple_of((block * heads + head) * BLOCK, BLOCK), BLOCK)
            key_cols = slice(head * KH, (head + 1) * KH)
            value_cols = slice(head * VH, (head + 1) * VH)
            inverse_ref[at, :] = inverses[head]
            pseudo = mm_out(inverses[head], beta * value)
            correct = mm_out(inverses[head], (beta * initial) * key)
            tail_key = tail * key
            step = jnp.where(row == column, end, 0.0) - mm_chain(tail_key, correct, TN)
            pseudo_ref[rows, value_cols] = pseudo
            correct_ref[rows, key_cols] = correct
            step_ref[at, :] = step
            add_ref[at, :] = mm_chain(tail_key, pseudo, TN)
            query_ref[rows, key_cols] = query
        return 0

    lax.fori_loop(0, blocks, first, 0)

    def second(block, states):
        after = []
        for head in range(heads):
            at = pl.ds(pl.multiple_of((block * heads + head) * BLOCK, BLOCK), BLOCK)
            state_ref[at, :] = states[head]
            after.append(mm_chain(step_ref[at, :], states[head]) + add_ref[at, :])
        return tuple(after)

    lax.fori_loop(
        0, blocks, second, tuple(jnp.zeros((KH, VH), jnp.float32) for _ in range(heads))
    )

    def third(block, _):
        start = pl.multiple_of(block * BLOCK, BLOCK)
        rows = pl.ds(start, BLOCK)
        for head in range(heads):
            at = pl.ds(pl.multiple_of((block * heads + head) * BLOCK, BLOCK), BLOCK)
            key_cols = slice(head * KH, (head + 1) * KH)
            value_cols = slice(head * VH, (head + 1) * VH)
            state = state_ref[at, :]
            score = score_ref[at, :]
            correct = correct_ref[rows, key_cols]
            query = query_ref[rows, key_cols]
            delta = pseudo_ref[rows, value_cols] - mm_out(correct, state)
            result = mm_out(query, state) + mm_out(score, delta)
            delta_ref[rows, value_cols] = delta
            result_ref[rows, value_cols] = result
            query_ref[rows, key_cols] = query - mm_out(score, correct)
            gate = proj_ref[
                rows, 2 * key_dim + value_dim + head * VH : 2 * key_dim + value_dim + (head + 1) * VH
            ]
            scale = lax.rsqrt(jnp.mean(result * result, axis=-1, keepdims=True) + out_epsilon)
            mixed = result * scale * gain_ref[...] * (gate * sigmoid(gate))
            mixed_ref[rows, value_cols] = mixed.astype(mixed_ref.dtype)
        return 0

    lax.fori_loop(0, blocks, third, 0)


def backward_kernel(
    heads,
    lengths_ref,
    grad_ref,
    proj_ref,
    filter_ref,
    decay_ref,
    gain_ref,
    act_ref,
    inverse_ref,
    state_ref,
    delta_ref,
    result_ref,
    score_ref,
    gram_ref,
    query_ref,
    step_ref,
    out_ref,
    filter_grad_ref,
    decay_grad_ref,
    gain_grad_ref,
    back_ref,
    reach_ref,
    act_grad_ref,
):
    length = proj_ref.shape[0]
    blocks = length // BLOCK
    key_dim, value_dim = heads * KH, heads * VH
    gate_at = 2 * key_dim + value_dim
    tail_at = 2 * key_dim + 2 * value_dim
    filter_grad_ref[...] = jnp.zeros_like(filter_grad_ref)
    decay_grad_ref[...] = jnp.zeros_like(decay_grad_ref)
    gain_grad_ref[...] = jnp.zeros_like(gain_grad_ref)
    act_grad_ref[length : length + 8, :] = jnp.zeros((8, gate_at), jnp.float32)

    def first(block, _):
        start = pl.multiple_of(block * BLOCK, BLOCK)
        rows = pl.ds(start, BLOCK)
        for head in range(heads):
            at = pl.ds(pl.multiple_of((block * heads + head) * BLOCK, BLOCK), BLOCK)
            key_cols = slice(head * KH, (head + 1) * KH)
            value_cols = slice(head * VH, (head + 1) * VH)
            gate_cols = slice(gate_at + head * VH, gate_at + (head + 1) * VH)
            result = result_ref[rows, value_cols]
            gate = proj_ref[rows, gate_cols]
            grad = grad_ref[rows, value_cols]
            sigma = sigmoid(gate)
            scale = lax.rsqrt(jnp.mean(result * result, axis=-1, keepdims=True) + out_epsilon)
            normed = result * scale
            out_ref[rows, gate_cols] = (
                grad * normed * gain_ref[...] * (sigma * (1.0 + gate * (1.0 - sigma)))
            ).astype(out_ref.dtype)
            grad = grad * (gate * sigma)
            gain_grad_ref[0:1, :] += jnp.sum(grad * normed, axis=0, keepdims=True)
            grad = grad * gain_ref[...]
            grad = scale * (grad - normed * jnp.mean(grad * normed, axis=-1, keepdims=True))
            back_ref[rows, value_cols] = grad
            reach_ref[at, :] = mm_chain(query_ref[rows, key_cols], grad, TN)
        return 0

    lax.fori_loop(0, blocks, first, 0)

    def second(index, states):
        block = blocks - 1 - index
        after = []
        for head in range(heads):
            at = pl.ds(pl.multiple_of((block * heads + head) * BLOCK, BLOCK), BLOCK)
            reach = reach_ref[at, :]
            reach_ref[at, :] = states[head]
            after.append(mm_chain(step_ref[at, :], states[head], TN) + reach)
        return tuple(after)

    lax.fori_loop(
        0, blocks, second, tuple(jnp.zeros((KH, VH), jnp.float32) for _ in range(heads))
    )

    def third(block, _):
        start = pl.multiple_of(block * BLOCK, BLOCK)
        rows = pl.ds(start, BLOCK)
        since, linked, strict, carried, tail_mask, last_carried = block_masks(lengths_ref, start)
        tail_tile = proj_ref[rows, tail_at : tail_at + TAIL]
        rate, logits = decays(tail_tile, decay_ref[0:1, :], decay_ref[1:2, :])
        beta_tile = sigmoid(tail_tile)
        cumulative = mm_sum(lower_ones(), rate)
        flipped = cumulative.T
        lane = lax.broadcasted_iota(jnp.int32, (BLOCK, TAIL), 1)
        place = lax.broadcasted_iota(jnp.int32, (BLOCK, TAIL), 0)
        cum_grad = jnp.zeros((BLOCK, TAIL), jnp.float32)
        cum_across = jnp.zeros((TAIL, BLOCK), jnp.float32)
        beta_grad = jnp.zeros((BLOCK, TAIL), jnp.float32)
        for head in range(heads):
            at = pl.ds(pl.multiple_of((block * heads + head) * BLOCK, BLOCK), BLOCK)
            key_cols = slice(head * KH, (head + 1) * KH)
            key_act = slice(key_dim + head * KH, key_dim + (head + 1) * KH)
            value_act = slice(2 * key_dim + head * VH, 2 * key_dim + (head + 1) * VH)
            value_cols = slice(head * VH, (head + 1) * VH)
            within, initial, tail, end = head_decay(
                cumulative, flipped, head, linked, carried, tail_mask, last_carried
            )
            beta = beta_tile[:, heads + head : heads + head + 1]
            summed = act_ref[rows, key_cols]
            query_sigma = sigmoid(summed)
            query = summed * query_sigma
            query_slope = query_sigma * (1.0 + summed * (1.0 - query_sigma))
            summed = act_ref[rows, key_act]
            key_sigma = sigmoid(summed)
            key = summed * key_sigma
            key_slope = key_sigma * (1.0 + summed * (1.0 - key_sigma))
            key_scale = lax.rsqrt(jnp.sum(key * key, axis=-1, keepdims=True) + epsilon)
            key = key * key_scale
            summed = act_ref[rows, value_act]
            value_sigma = sigmoid(summed)
            value = summed * value_sigma
            value_slope = value_sigma * (1.0 + summed * (1.0 - value_sigma))
            grad = back_ref[rows, value_cols]
            after = reach_ref[at, :]
            state = state_ref[at, :]
            score = score_ref[at, :]
            gram = gram_ref[at, :]
            delta = delta_ref[rows, value_cols]
            tail_key = tail * key
            delta_grad = mm_back(score, grad, TN) + mm_back(tail_key, after)
            scaled_grad = mm_back(inverse_ref[at, :], delta_grad, TN)
            pair = jnp.concatenate([grad, scaled_grad], axis=0)
            by_state = mm_back(pair, state, NT)
            query_grad = by_state[:BLOCK]
            written_grad = -by_state[BLOCK:]
            by_delta = mm_back(pair, delta, NT)
            tail_grad = mm_back(delta, after, NT)
            score_grad = by_delta[:BLOCK]
            lower_grad = -by_delta[BLOCK:]
            initial_key = initial * key
            beta_one = (
                jnp.sum(scaled_grad * value, axis=-1, keepdims=True)
                + jnp.sum(written_grad * initial_key, axis=-1, keepdims=True)
                + jnp.sum(lower_grad * gram, axis=-1, keepdims=True)
            )
            spread_grad = score_grad * score + lower_grad * (beta * gram)
            tail_one = tail * jnp.sum(tail_grad * key, axis=-1, keepdims=True)
            initial_one = initial * (
                jnp.sum(query_grad * query, axis=-1, keepdims=True)
                + beta * jnp.sum(written_grad * key, axis=-1, keepdims=True)
            )
            last_one = jnp.sum(tail_one, axis=0, keepdims=True) + end * jnp.sum(
                jnp.sum(state * after, axis=-1, keepdims=True), axis=0, keepdims=True
            )
            cum_one = jnp.sum(spread_grad, axis=-1, keepdims=True) + initial_one - tail_one
            cum_grad = cum_grad + jnp.where(lane == head, cum_one, 0.0)
            cum_grad = cum_grad + jnp.where((lane == head) & (place == BLOCK - 1), last_one, 0.0)
            cum_across = cum_across + jnp.where(
                place == head, jnp.sum(spread_grad, axis=0, keepdims=True), 0.0
            )
            beta_grad = beta_grad + jnp.where(lane == heads + head, beta_one, 0.0)
            score_grad = score_grad * within
            gram_grad = jnp.where(strict, lower_grad * within, 0.0) * beta
            by_key = mm_back(jnp.concatenate([score_grad, gram_grad], axis=0), key)
            query_grad = initial * query_grad + by_key[:BLOCK]
            key_grad = (
                (beta * initial) * written_grad
                + tail * tail_grad
                + by_key[BLOCK:]
                + mm_back(gram_grad, key, TN)
                + mm_back(score_grad, query, TN)
            )
            key_grad = key_scale * (
                key_grad - key * jnp.sum(key_grad * key, axis=-1, keepdims=True)
            )
            act_grad_ref[rows, key_cols] = query_grad * query_slope
            act_grad_ref[rows, key_act] = key_grad * key_slope
            act_grad_ref[rows, value_act] = (beta * scaled_grad) * value_slope
        cum_grad = cum_grad - cum_across.T
        rate_grad = mm_sum(lower_ones(), cum_grad, TN)
        logit_grad = rate_grad * (-jnp.exp(decay_ref[0:1, :])) * sigmoid(logits)
        decay_grad_ref[0:1, :] += jnp.sum(rate_grad * rate, axis=0, keepdims=True)
        decay_grad_ref[1:2, :] += jnp.sum(logit_grad, axis=0, keepdims=True)
        out_ref[rows, tail_at : tail_at + TAIL] = jnp.where(
            lane < heads, logit_grad, beta_grad * beta_tile * (1.0 - beta_tile)
        ).astype(out_ref.dtype)
        return 0

    lax.fori_loop(0, blocks, third, 0)

    def fourth(block, _):
        start = pl.multiple_of(block * BLOCK, BLOCK)
        rows = pl.ds(start, BLOCK)
        positions = start + lax.broadcasted_iota(jnp.int32, (BLOCK + 8, 1), 0)
        since = positions - document_starts(lengths_ref, positions)
        for low, high in (
            (0, key_dim),
            (key_dim, 2 * key_dim),
            (2 * key_dim, 2 * key_dim + value_dim),
        ):
            columns = slice(low, high)
            later = jnp.concatenate(
                [
                    act_grad_ref[rows, columns],
                    act_grad_ref[pl.ds(pl.multiple_of(start + BLOCK, 8), 8), columns],
                ],
                axis=0,
            )
            seen = window_before(proj_ref, start, columns)
            here = later[:BLOCK]
            summed = here * filter_ref[CONV - 1 : CONV, columns]
            filter_grad_ref[CONV - 1 : CONV, columns] += jnp.sum(
                here * seen[8:], axis=0, keepdims=True
            )
            for offset in range(1, CONV):
                tap = CONV - 1 - offset
                mask = (since >= offset).astype(jnp.float32)
                summed = summed + later[offset : offset + BLOCK] * (
                    mask[offset : offset + BLOCK] * filter_ref[tap : tap + 1, columns]
                )
                filter_grad_ref[tap : tap + 1, columns] += jnp.sum(
                    here * (mask[:BLOCK] * seen[8 - offset : 8 - offset + BLOCK]),
                    axis=0,
                    keepdims=True,
                )
            out_ref[rows, columns] = summed.astype(out_ref.dtype)
        return 0

    lax.fori_loop(0, blocks, fourth, 0)


def f32(*shape):
    return jax.ShapeDtypeStruct(shape, jnp.float32)


VMEM = pl.BlockSpec(memory_space=pltpu.VMEM)
SMEM = pl.BlockSpec(memory_space=pltpu.SMEM)
PARAMS = pltpu.CompilerParams(vmem_limit_bytes=60 * 2**20)


def mixer_forward(lengths, proj, filters, decay_pair, out_gain, heads):
    length = proj.shape[0]
    pairs = length // BLOCK * heads * BLOCK
    key_dim, value_dim = heads * KH, heads * VH
    return pl.pallas_call(
        functools.partial(forward_kernel, heads),
        out_shape=(
            jax.ShapeDtypeStruct((length, value_dim), jnp.bfloat16),
            f32(length, 2 * key_dim + value_dim),
            f32(pairs, BLOCK),
            f32(pairs, VH),
            f32(length, value_dim),
            f32(length, value_dim),
            f32(pairs, BLOCK),
            f32(pairs, BLOCK),
            f32(length, key_dim),
            f32(pairs, KH),
        ),
        in_specs=[SMEM] + [VMEM] * 4,
        out_specs=(VMEM,) * 10,
        scratch_shapes=[
            pltpu.VMEM((length, value_dim), jnp.float32),
            pltpu.VMEM((length, key_dim), jnp.float32),
            pltpu.VMEM((pairs, VH), jnp.float32),
        ],
        compiler_params=PARAMS,
        cost_estimate=pl.CostEstimate(
            flops=30 * 10**9, bytes_accessed=24 * 2**20, transcendentals=0
        ),
        name="mixer_forward",
    )(lengths, proj, filters, decay_pair, out_gain)


def mixer_backward(lengths, grad, proj, filters, decay_pair, out_gain, kept, heads):
    length = proj.shape[0]
    pairs = length // BLOCK * heads * BLOCK
    key_dim, value_dim = heads * KH, heads * VH
    return pl.pallas_call(
        functools.partial(backward_kernel, heads),
        out_shape=(
            jax.ShapeDtypeStruct(proj.shape, jnp.bfloat16),
            f32(CONV, 2 * key_dim + value_dim),
            f32(8, TAIL),
            f32(8, VH),
        ),
        in_specs=[SMEM] + [VMEM] * (5 + len(kept)),
        out_specs=(VMEM,) * 4,
        scratch_shapes=[
            pltpu.VMEM((length, value_dim), jnp.float32),
            pltpu.VMEM((pairs, VH), jnp.float32),
            pltpu.VMEM((length + 8, 2 * key_dim + value_dim), jnp.float32),
        ],
        compiler_params=PARAMS,
        cost_estimate=pl.CostEstimate(
            flops=30 * 10**9, bytes_accessed=32 * 2**20, transcendentals=0
        ),
        name="mixer_backward",
    )(lengths, grad, proj, filters, decay_pair, out_gain, *kept)


def plain_product(first_mat, second_mat):
    return jnp.dot(first_mat, second_mat, preferred_element_type=jnp.float32)


def left_product(first_mat, second_mat):
    return lax.dot_general(first_mat, second_mat, TN, preferred_element_type=jnp.float32)


def right_product(first_mat, second_mat):
    return lax.dot_general(first_mat, second_mat, NT, preferred_element_type=jnp.float32)


def rms_scale(values, scales):
    return values * lax.rsqrt(jnp.mean(values * values, axis=-1, keepdims=True) + epsilon) * scales


def norm_back(inputs, scales, grad_normed):
    inverse = lax.rsqrt(jnp.mean(inputs * inputs, axis=-1, keepdims=True) + epsilon)
    weighted = scales * grad_normed
    grad_inputs = inverse * weighted - inputs * (inverse * inverse * inverse) * jnp.mean(
        weighted * inputs, axis=-1, keepdims=True
    )
    grad_scales = jnp.sum(grad_normed * inputs * inverse, axis=0)
    return (grad_inputs, grad_scales)


def swap(values, axis):
    return lax.ppermute(values, axis, [(0, 1), (1, 0)])


def joined(own, other, axis):
    leads = lax.axis_index(axis) == 0
    return jnp.concatenate(
        [jnp.where(leads, own, other), jnp.where(leads, other, own)], axis=1
    )


def gather_features(own):
    half = joined(own, swap(own, "col"), "col")
    return joined(half, swap(half, "row"), "row")


def half_of(values, index):
    width = values.shape[1] // 2
    return lax.dynamic_slice_in_dim(values, index * width, width, 1)


def scatter_features(partial):
    for axis in ("row", "col"):
        index = lax.axis_index(axis)
        other = swap(half_of(partial, 1 - index).astype(jnp.bfloat16), axis)
        partial = half_of(partial, index) + other.astype(jnp.float32)
    return partial


def body(
    tokens,
    cotangent,
    lengths,
    norm_gain,
    w_query,
    w_key,
    w_value,
    w_alpha,
    w_beta,
    conv_query,
    conv_key,
    conv_value,
    decay_log,
    decay_bias,
    w_outgate,
    out_gain,
    w_out,
    ffn_gain,
    w_gate,
    w_up,
    w_down,
):
    heads = w_alpha.shape[1]
    key_dim, value_dim = heads * KH, heads * VH
    small = jnp.zeros((w_alpha.shape[0], TAIL - 2 * heads), w_alpha.dtype)
    weights = jnp.concatenate([w_query, w_key, w_value, w_outgate, w_alpha, w_beta, small], axis=1)
    filters = jnp.concatenate([conv_query, conv_key, conv_value], axis=1)
    decay_pair = jnp.pad(jnp.stack([decay_log, decay_bias]), ((0, 6), (0, TAIL - heads)))
    gain_row = out_gain[None]

    whole = gather_features(tokens).astype(jnp.float32)
    grad_out = gather_features(cotangent)
    normed = rms_scale(whole, norm_gain).astype(jnp.bfloat16)
    proj = plain_product(normed, weights)
    mixed, *kept = mixer_forward(lengths, proj, filters, decay_pair, gain_row, heads)
    hidden_own = tokens.astype(jnp.float32) + scatter_features(plain_product(mixed, w_out))
    hidden = gather_features(hidden_own)
    normed_ffn = rms_scale(hidden, ffn_gain).astype(jnp.bfloat16)
    gate_act = plain_product(normed_ffn, w_gate)
    up_act = plain_product(normed_ffn, w_up)
    sigma = jax.nn.sigmoid(gate_act)
    product = (gate_act * sigma * up_act).astype(jnp.bfloat16)
    grad_product = right_product(grad_out, w_down)
    grad_gate_act = (grad_product * up_act * sigma * (1.0 + gate_act * (1.0 - sigma))).astype(
        jnp.bfloat16
    )
    grad_up_act = (grad_product * gate_act * sigma).astype(jnp.bfloat16)
    grad_normed_ffn = right_product(grad_gate_act, w_gate) + right_product(grad_up_act, w_up)
    grad_hidden_part, grad_ffn_gain = norm_back(hidden, ffn_gain, grad_normed_ffn)
    grad_down = left_product(product, grad_out)
    grad_gate = left_product(normed_ffn, grad_gate_act)
    grad_up = left_product(normed_ffn, grad_up_act)
    ffn_sums = lax.psum(
        tuple(item.astype(jnp.bfloat16) for item in (grad_down, grad_gate, grad_up)), "dp"
    )
    grad_hidden_own = (
        cotangent.astype(jnp.float32) + scatter_features(grad_hidden_part)
    ).astype(jnp.bfloat16)
    grad_hidden = gather_features(grad_hidden_own)
    output = (hidden_own + scatter_features(plain_product(product, w_down))).astype(jnp.bfloat16)
    grad_mixed = right_product(grad_hidden, w_out)
    grad_proj, filter_grad, decay_grad, gain_grad = mixer_backward(
        lengths, grad_mixed, proj, filters, decay_pair, gain_row, tuple(kept), heads
    )
    grad_normed = right_product(grad_proj, weights)
    grad_input_part, grad_norm_gain = norm_back(whole, norm_gain, grad_normed)
    grad_out_proj = left_product(mixed, grad_hidden)
    grad_weights = left_product(normed, grad_proj)
    tail_at = 2 * key_dim + 2 * value_dim
    mixer_sums = lax.psum(
        (
            grad_out_proj.astype(jnp.bfloat16),
            grad_weights[:, :tail_at].astype(jnp.bfloat16),
        ),
        "dp",
    )
    input_grad = (
        grad_hidden_own.astype(jnp.float32) + scatter_features(grad_input_part)
    ).astype(jnp.bfloat16)
    gains = lax.psum(
        jnp.concatenate([grad_norm_gain, grad_ffn_gain, gain_grad[0]]), ("row", "col")
    )
    sizes = (
        gains,
        filter_grad.reshape(-1),
        grad_weights[:, tail_at : tail_at + 2 * heads].reshape(-1),
        decay_grad[:2, :heads].reshape(-1),
    )
    small_sum = lax.psum(jnp.concatenate(sizes), "dp")
    width = norm_gain.shape[0]
    places = [0]
    for item in sizes:
        places.append(places[-1] + item.shape[0])
    pieces = [small_sum[low:high] for low, high in zip(places, places[1:])]
    filter_sum = pieces[1].reshape(filters.shape)
    pair_sum = pieces[2].reshape(-1, 2 * heads)
    decay_sum = pieces[3].reshape(2, heads)
    down_sum, gate_sum, up_sum = (item.astype(jnp.float32) for item in ffn_sums)
    out_sum, weight_sum = (item.astype(jnp.float32) for item in mixer_sums)
    return (
        output,
        input_grad,
        pieces[0][:width],
        weight_sum[:, :key_dim],
        weight_sum[:, key_dim : 2 * key_dim],
        weight_sum[:, 2 * key_dim : 2 * key_dim + value_dim],
        pair_sum[:, :heads],
        pair_sum[:, heads:],
        filter_sum[:, :key_dim],
        filter_sum[:, key_dim : 2 * key_dim],
        filter_sum[:, 2 * key_dim :],
        decay_sum[0],
        decay_sum[1],
        weight_sum[:, 2 * key_dim + value_dim :],
        pieces[0][2 * width :],
        out_sum,
        pieces[0][width : 2 * width],
        gate_sum,
        up_sum,
        down_sum,
    )


def solution(mesh):
    placed = (
        P("dp", ("row", "col")),
        P("dp", ("row", "col")),
        P("dp", None),
        P(),
        P(None, ("row", "col")),
        P(None, ("row", "col")),
        P(None, ("row", "col")),
        P(None, ("row", "col")),
        P(None, ("row", "col")),
        P(None, ("row", "col")),
        P(None, ("row", "col")),
        P(None, ("row", "col")),
        P(("row", "col")),
        P(("row", "col")),
        P(None, ("row", "col")),
        P(),
        P(("row", "col"), None),
        P(),
        P(None, ("row", "col")),
        P(None, ("row", "col")),
        P(("row", "col"), None),
    )
    return jax.shard_map(
        body,
        mesh=mesh,
        in_specs=placed,
        out_specs=(
            P("dp", ("row", "col")),
            P("dp", ("row", "col")),
            P(),
            P(None, ("row", "col")),
            P(None, ("row", "col")),
            P(None, ("row", "col")),
            P(None, ("row", "col")),
            P(None, ("row", "col")),
            P(None, ("row", "col")),
            P(None, ("row", "col")),
            P(None, ("row", "col")),
            P(("row", "col")),
            P(("row", "col")),
            P(None, ("row", "col")),
            P(),
            P(("row", "col"), None),
            P(),
            P(None, ("row", "col")),
            P(None, ("row", "col")),
            P(("row", "col"), None),
        ),
        check_vma=False,
    )
```

time: 1880 us -> 585 us (0.31)
  other arithmetic: 492 us -> 32.6 us
  matrix products: 472 us -> 49.9 us
  waiting for transfers between devices: 592 us -> 275 us
  local copies, waits for them, and re-layouts: 206 us -> 48.5 us
  Pallas kernels: 0 us -> 87.5 us
  blocking collectives: 84.3 us -> 52.9 us
    dot_general x220 -> x10, matrix products: 428 us -> 34.1 us  [the longest x5 17.3 us: right_product(): lax.dot_general(first_mat, second_mat, NT, preferred_element_type=jnp.flo...]
    another operation x11 -> x1, other arithmetic: 325 us -> 0.6 us  [body(): jnp.stack([decay_log, decay_bias])]
    psum x1, waiting for transfers between devices: 452 us -> 182 us  [body(): lax.psum((grad_out_proj.astype(jnp.bfloat16), grad_weights[:, :tail_at].a...]
    ppermute x0 -> x16, waiting for transfers between devices: none -> 93.6 us  [swap(): return lax.ppermute(values, axis, [(0, 1), (1, 0)])]
    pallas_call x0 -> x2, Pallas kernels: none -> 87.5 us  [the longest x1 44.7 us: mixer_backward(): pl.pallas_call(functools.partial(backward_kernel, heads), out_shape=(jax....]
    reduce_scatter x4 -> x0, waiting for transfers between devices: 76.2 us -> none  [the longest x1 44.6 us: body(): lax.psum_scatter(partial_out, ('row', 'col'), scatter_dimension=1, tiled=...]
    all_gather x4 -> x0, waiting for transfers between devices: 62.2 us -> none  [the longest x1 34 us: body(): hidden = lax.all_gather(hidden_own, ('row', 'col'), axis=1, tiled=True)]
    reduce_sum x42 -> x0, other arithmetic: 54.2 us -> none  [the longest x16 17.4 us: advance(): end_c[..., None, None] * memory]
  transfers between devices with their start and end apart: 9 -> 17, of which waited for: 6 -> 12; matrix products, arithmetic and copies ran while one was open for 34% -> 10% of each run, Pallas kernels for 0% -> 0%
where the time goes in v1:
time: 585 us; the launch traced here: 577 us
  waiting for transfers between devices  275 us (47%)
  Pallas kernels  87.5 us (15%)
  blocking collectives  52.9 us (9%)
  matrix products  49.9 us (9%)
  local copies, waits for them, and re-layouts  48.5 us (8%)
  other arithmetic  32.6 us (6%)
  starting transfers between devices  15.2 us (3%)
  between operations  15 us (3%)
    psum x1, waiting for transfers between devices, body(): lax.psum((grad_out_proj.astype(jnp.bfloat16), grad_weights[:, :tail_at].a...  182 us
    ppermute x16, waiting for transfers between devices, swap(): return lax.ppermute(values, axis, [(0, 1), (1, 0)])  93.6 us
    pallas_call x1, Pallas kernels, mixer_backward(): pl.pallas_call(functools.partial(backward_kernel, heads), out_shape=(jax....  44.7 us
    pallas_call x1, Pallas kernels, mixer_forward(): pl.pallas_call(functools.partial(forward_kernel, heads), out_shape=(jax.S...  42.7 us
    psum x1, blocking collectives, body(): small_sum = lax.psum(jnp.concatenate(sizes), 'dp')  40.3 us
    unnamed x109, local copies, waits for them, and re-layouts  20.1 us
    dot_general x5, matrix products, right_product(): lax.dot_general(first_mat, second_mat, NT, preferred_element_type=jnp.flo...  17.3 us
    dot_general x5, matrix products, left_product(): lax.dot_general(first_mat, second_mat, TN, preferred_element_type=jnp.flo...  16.8 us
  transfers between devices with their start and end apart: 17, of which 12 were waited for; matrix products, arithmetic and copies ran while one was open for 10% of the time, Pallas kernels for 0%

profile of v1, /device:TPU:0, one launch (start us, length us, event | category | flops | bytes accessed | tf_op | source)
XLA Modules:
  0.0 577.1 jit_solution(9568854704619039256)
XLA Ops:
  8.6 3.0 collective-permute-start.8
  13.1 11.4 %collective-permute-done.8 = bf16[1024,256]{0,1:T(8,128)(2,1)} collective-permute-done((bf16[1024,256]{0,1:T(8,128)(2,1)S(1)}, bf16[1024,256]{0,1:T(8,128)(2,1)}, u32[]{:S(2)}, u32[]{:S(2)}) %collective-permute-start.8) | collective-permute-done | bytes 524320 | tf_op jit(solution)/shard_map/ppermute | solution.py:601
  26.9 8.0 %collective-permute-done = bf16[1024,256]{0,1:T(8,128)(2,1)} collective-permute-done((bf16[1024,256]{0,1:T(8,128)(2,1)S(1)}, bf16[1024,256]{0,1:T(8,128)(2,1)}, u32[]{:S(2)}, u32[]{:S(2)}) %collective-permute-start) | collective-permute-done | bytes 524320 | tf_op jit(solution)/shard_map/ppermute | solution.py:601
  37.9 6.6 %concatenate.38 = bf16[1024,1664]{1,0:T(8,128)(2,1)} concatenate(bf16[1024,256]{1,0:T(8,128)(2,1)} %param.25, bf16[1024,256]{1,0:T(8,128)(2,1)} %param.26, bf16[1024,512]{1,0:T(8,128)(2,1)} %param.27, bf16[1024,512]{1,0:T(8,128)(2,1)} %param.35, bf16[1024,2]{1,0:T(8,128)(2,1)S(1)} %copy.61, bf16[1024,2]{1,0:T(8,128)(2,1)S(1)} %copy.62, bf16[1024,124]{1,0:T(8,128)(2,1)S(1)} %broadcast_in_dim.4), dimensions={1} | concatenate | bytes 6815744 | tf_op jit(solution)/shard_map/concatenate | solution.py:655
  45.2 4.9 broadcast_select_fusion.3
  51.2 6.4 %fusion.12.proj_ref = f32[1024,1664]{1,0:T(8,128)} fusion(bf16[1024,1664]{1,0:T(8,128)(2,1)S(1)} %copy-done.14, f32[1024]{0:T(1024)S(1)} %copy-done.29, f32[1024]{0:T(1024)S(1)} %get-tuple-element.131, bf16[1024,512]{0,1:T(8,128)(2,1)S(1)} %get-tuple-element.136, bf16[1024,512]{0,1:T(8,128)(2,1)S(1)} %get-tuple-element.137), kind=kOutput, calls=%fused_computation.63 | convolution fusion | flops 3497000960 | bytes 12328960 | tf_op jit(solution)/shard_map/dot_general | solution.py:575
  57.6 42.7 %mixer_forward.1 = (bf16[1024,512]{1,0:T(8,128)(2,1)}, f32[1024,1024]{1,0:T(8,128)}, f32[2048,128]{1,0:T(8,128)}, f32[2048,256]{1,0:T(8,128)}, f32[1024,512]{1,0...) custom-call(s32[1,4]{1,0:T(1,128)} %lengths_ref.3, ...), custom_call_target="tpu_custom_call" | custom-call | flops 30000001024 | bytes 25165824 | tf_op jit(solution)/shard_map/mixer_forward/pallas_call | solution.py:518
  100.3 2.9 fusion.25
  106.7 2.6 collective-permute-done.2
  115.5 12.8 %collective-permute-done.3 = bf16[1024,256]{0,1:T(8,128)(2,1)} collective-permute-done((bf16[1024,256]{0,1:T(8,128)(2,1)}, bf16[1024,256]{0,1:T(8,128)(2,1)}, u32[]{:S(2)}, u32[]{:S(2)}) %collective-permute-start.3) | collective-permute-done | bytes 524320 | tf_op jit(solution)/shard_map/ppermute | solution.py:601
  131.8 22.9 %collective-permute-done.4 = f32[1024,256]{0,1:T(8,128)S(1)} collective-permute-done((f32[1024,256]{0,1:T(8,128)S(1)}, f32[1024,256]{0,1:T(8,128)S(1)}, u32[]{:S(2)}, u32[]{:S(2)}) %collective-permute-start.4) | collective-permute-done | bytes 1048608 | tf_op jit(solution)/shard_map/ppermute | solution.py:601
  155.1 4.1 collective-permute-done.5
  165.6 4.3 multiply_convert_fusion.1
  171.9 3.4 multiply_reduce_fusion
  176.4 2.5 collective-permute-done.10
  181.1 12.2 %collective-permute-done.11 = bf16[1024,256]{0,1:T(8,128)(2,1)S(1)} collective-permute-done((bf16[1024,256]{0,1:T(8,128)(2,1)S(1)}, bf16[1024,256]{0,1:T(8,128)(2,1)S(1)}, u32[]{:S(2)}, u32[]{:S(2)}) %collective-permute-start.11) | collective-permute-done | bytes 524320 | tf_op jit(solution)/shard_map/ppermute | solution.py:601
  195.4 11.4 %collective-permute-done.12 = bf16[1024,256]{0,1:T(8,128)(2,1)S(1)} collective-permute-done((bf16[1024,256]{0,1:T(8,128)(2,1)S(1)}, bf16[1024,256]{0,1:T(8,128)(2,1)S(1)}, u32[]{:S(2)}, u32[]{:S(2)}) %collective-permute-start.12) | collective-permute-done | bytes 524320 | tf_op jit(solution)/shard_map/ppermute | solution.py:601
  207.1 2.8 convolution_convert_fusion
  209.9 2.8 convolution_convert_fusion.1
  212.7 2.8 convolution_convert_fusion.2
  219.2 2.6 fusion.8.grad_ref
  221.8 44.7 %mixer_backward.1 = (bf16[1024,1664]{1,0:T(8,128)(2,1)}, f32[4,1024]{1,0:T(4,128)}, f32[8,128]{1,0:T(8,128)}, f32[8,256]{1,0:T(8,128)}) custom-call(s32[1,4]{1,0:T(1,128)} %lengths_ref.3, f32[1024,512]{1,0:T(8,128)} %fusion.8.grad_ref, f32[1024,1664]{1,0:T(8,128)} %fusion.12.proj_ref, f32[4,1024]{1,0:T(4,128)} %copy-done.36, ...), custom_call_target="tpu_custom_call" | custom-call | flops 30000001024 | bytes 33554432 | tf_op jit(solution)/shard_map/mixer_backward/pallas_call | solution.py:551
  266.5 6.0 %fusion.10 = f32[1024,1664]{1,0:T(8,128)S(1)} fusion(bf16[1024,1664]{1,0:T(8,128)(2,1)} %get-tuple-element.44, f32[1024]{0:T(1024)S(1)} %copy-done.29, f32[1024]{0:T(1024)S(1)} %get-tuple-element.131, bf16[1024,512]{0,1:T(8,128)(2,1)S(1)} %get-tuple-element.136, bf16[1024,512]{0,1:T(8,128)(2,1)S(1)} %get-tuple-element.137), kind=kOutput, calls=%fused_computation.62 | convolution fusion | flops 3497000960 | bytes 12328960 | tf_op jit(solution)/shard_map/dot_general | solution.py:579
  272.5 2.8 copy-done.17
  277.3 3.3 fusion.26
  285.8 5.0 fusion.7
  295.0 3.3 collective-permute-done.7
  301.3 12.6 %psum.49 = f32[2304]{0:T(1024)S(1)} all-reduce(f32[2304]{0:T(1024)S(1)} %pad_maximum_fusion.13), channel_id=1, replica_groups=mesh['dp'=8,'row'=2,'col'=2] {'row','col'}, use_global_device_ids=true, to_apply=%region_6.7 | all-reduce | flops 2304 | bytes 18432 | tf_op jit(solution)/shard_map/psum | solution.py:709
  314.0 40.3 %psum.50 = f32[10500]{0:T(1024)S(1)} all-reduce(f32[10500]{0:T(1024)S(1)} %pad_maximum_fusion.12), channel_id=1, replica_groups=mesh['dp'=8,'row'=2,'col'=2] {'dp'}, use_global_device_ids=true, to_apply=%region_7.8 | all-reduce | flops 10500 | bytes 84000 | tf_op jit(solution)/shard_map/psum | solution.py:718
  375.1 181.9 %all-reduce.4.cloned.1.call-done = (bf16[1024,1536]{1,0:T(8,128)(2,1)}, bf16[512,1024]{1,0:T(8,128)(2,1)}, bf16[1024,704]{0,1:T(8,128)(2,1)}, bf16[1024,704]{0,1:T(8,128)(2,1)}, bf16[704,1024]{1,0:T(8,128)(2,1)}) async-done(((bf16[1024,1536]{1,0:T(8,128)(2,1)}, bf16[512,1024]{1,0:T(8,128)(2,1)}, bf16[1024,704]{0,1:T(8,128)(2,1)}, bf16[1024,704]{0,1:T(8,128)(2,1)}, bf16[704,1024]{1,0:T(8,128)(2,1)}), ...) | async-done | bytes 8519696 | tf_op jit(solution)/shard_map/psum | solution.py:699
  557.0 2.8 fusion.19
  559.8 2.6 fusion.18
  (195 shorter events, 83.6 us)
Async XLA Ops:
  7.2 158.4 %copy-start = (bf16[704,1024]{1,0:T(8,128)(2,1)S(1)}, bf16[704,1024]{1,0:T(8,128)(2,1)}, u32[]{:S(2)}) copy-start(bf16[704,1024]{1,0:T(8,128)(2,1)} %param.41) | copy-start | bytes 4325380
  7.2 549.7 %all-reduce.4.cloned.1.call-start = ((), (), s32[]{:S(2)}) async-start(), calls=%async_computation | async-start | bytes 17039360 | tf_op jit(solution)/shard_map/psum | solution.py:699
  8.6 18.2 %copy-start.10 = (bf16[1024,256]{0,1:T(8,128)(2,1)}, bf16[1024,256]{0,1:T(8,128)(2,1)S(1)}, u32[]{:S(2)}) copy-start(bf16[1024,256]{0,1:T(8,128)(2,1)S(1)} %copy.65) | copy-start | bytes 1572868
  8.6 15.9 %collective-permute-start.8 = (bf16[1024,256]{0,1:T(8,128)(2,1)S(1)}, bf16[1024,256]{0,1:T(8,128)(2,1)}, u32[]{:S(2)}, u32[]{:S(2)}) collective-permute-start(bf16[1024,256]{0,1:T(8,128)(2,1)S(1)} %copy.65), channel_id=1, source_target_pairs={{0,1},{1,0},{2,3},{3,2},{4,5},{5,4},{6,7},{7,6},{8,9},{9,8},{10,11... | collective-permute-start | bytes 1572872 | tf_op jit(solution)/shard_map/ppermute | solution.py:601
  12.9 13.9 %copy-start.12 = (bf16[1024,256]{0,1:T(8,128)(2,1)}, bf16[1024,256]{0,1:T(8,128)(2,1)S(1)}, u32[]{:S(2)}) copy-start(bf16[1024,256]{0,1:T(8,128)(2,1)S(1)} %copy.57) | copy-start | bytes 1572868
  12.9 22.0 %collective-permute-start = (bf16[1024,256]{0,1:T(8,128)(2,1)S(1)}, bf16[1024,256]{0,1:T(8,128)(2,1)}, u32[]{:S(2)}, u32[]{:S(2)}) collective-permute-start(bf16[1024,256]{0,1:T(8,128)(2,1)S(1)} %copy.57), channel_id=1, source_target_pairs={{0,1},{1,0},{2,3},{3,2},{4,5},{5,4},{6,7},{7,6},{8,9},{9,8},{10,11... | collective-permute-start | bytes 1572872 | tf_op jit(solution)/shard_map/ppermute | solution.py:601
  25.6 10.6 %copy-start.6 = (bf16[1024,256]{0,1:T(8,128)(2,1)}, bf16[1024,256]{0,1:T(8,128)(2,1)S(1)}, u32[]{:S(2)}) copy-start(bf16[1024,256]{0,1:T(8,128)(2,1)S(1)} %get-tuple-element.116) | copy-start | bytes 1572868
  25.6 10.6 %copy-start.7 = (bf16[1024,256]{0,1:T(8,128)(2,1)}, bf16[1024,256]{0,1:T(8,128)(2,1)S(1)}, u32[]{:S(2)}) copy-start(bf16[1024,256]{0,1:T(8,128)(2,1)S(1)} %get-tuple-element.117) | copy-start | bytes 1572868
  26.8 10.6 %copy-start.30 = (bf16[1024,2]{0,1:T(2,128)(2,1)S(1)}, bf16[1024,2]{0,1:T(2,128)(2,1)}, u32[]{:S(2)}) copy-start(bf16[1024,2]{0,1:T(2,128)(2,1)} %param.28) | copy-start | bytes 12292
  26.8 10.8 %copy-start.31 = (bf16[1024,2]{0,1:T(2,128)(2,1)S(1)}, bf16[1024,2]{0,1:T(2,128)(2,1)}, u32[]{:S(2)}) copy-start(bf16[1024,2]{0,1:T(2,128)(2,1)} %param.29) | copy-start | bytes 12292
  26.8 18.4 %collective-permute-start.9 = (bf16[1024,512]{0,1:T(8,128)(2,1)}, bf16[1024,512]{0,1:T(8,128)(2,1)}, u32[]{:S(2)}, u32[]{:S(2)}) collective-permute-start(bf16[1024,512]{0,1:T(8,128)(2,1)} %pad_maximum_fusion.10), channel_id=1, source_target_pairs={{0,2},{2,0},{1,3},{3,1},{4,6},{6,4},{5,7},{7,5},{8,10},{10,8},{9,1... | collective-permute-start | bytes 3145736 | tf_op jit(solution)/shard_map/ppermute | solution.py:601
  36.2 8.3 %copy-start.8 = (bf16[1024,256]{0,1:T(8,128)(2,1)}, bf16[1024,256]{0,1:T(8,128)(2,1)S(1)}, u32[]{:S(2)}) copy-start(bf16[1024,256]{0,1:T(8,128)(2,1)S(1)} %get-tuple-element.118) | copy-start | bytes 1572868
  36.2 8.3 %copy-start.9 = (bf16[1024,256]{0,1:T(8,128)(2,1)}, bf16[1024,256]{0,1:T(8,128)(2,1)S(1)}, u32[]{:S(2)}) copy-start(bf16[1024,256]{0,1:T(8,128)(2,1)S(1)} %get-tuple-element.119) | copy-start | bytes 1572868
  37.3 7.8 %collective-permute-start.1 = (bf16[1024,512]{0,1:T(8,128)(2,1)}, bf16[1024,512]{0,1:T(8,128)(2,1)}, u32[]{:S(2)}, u32[]{:S(2)}) collective-permute-start(bf16[1024,512]{0,1:T(8,128)(2,1)} %pad_maximum_fusion.9), channel_id=1, source_target_pairs={{0,2},{2,0},{1,3},{3,1},{4,6},{6,4},{5,7},{7,5},{8,10},{10,8},{9,1... | collective-permute-start | bytes 3145736 | tf_op jit(solution)/shard_map/ppermute | solution.py:601
  37.8 7.3 %copy-start.33 = (f32[4,256]{1,0:T(4,128)S(1)}, f32[4,256]{1,0:T(4,128)}, u32[]{:S(2)}) copy-start(f32[4,256]{1,0:T(4,128)} %param.31) | copy-start | bytes 12292
  37.8 7.3 %copy-start.28 = (f32[4,512]{1,0:T(4,128)S(1)}, f32[4,512]{1,0:T(4,128)}, u32[]{:S(2)}) copy-start(f32[4,512]{1,0:T(4,128)} %param.32) | copy-start | bytes 24580
  106.2 3.1 collective-permute-start.2
  113.8 14.5 %collective-permute-start.3 = (bf16[1024,256]{0,1:T(8,128)(2,1)}, bf16[1024,256]{0,1:T(8,128)(2,1)}, u32[]{:S(2)}, u32[]{:S(2)}) collective-permute-start(bf16[1024,256]{0,1:T(8,128)(2,1)} %dynamic-slice_convert_fusion.7), channel_id=1, source_target_pairs={{0,1},{1,0},{2,3},{3,2},{4,5},{5,4},{6,7},{7,6},{8,9},{9,8},{10,11... | collective-permute-start | bytes 1572872 | tf_op jit(solution)/shard_map/ppermute | solution.py:601
  130.0 24.9 %copy-start.3 = (f32[1024,256]{0,1:T(8,128)}, f32[1024,256]{0,1:T(8,128)S(1)}, u32[]{:S(2)}) copy-start(f32[1024,256]{0,1:T(8,128)S(1)} %add_add_fusion) | copy-start | bytes 3145732
  130.0 24.7 %collective-permute-start.4 = (f32[1024,256]{0,1:T(8,128)S(1)}, f32[1024,256]{0,1:T(8,128)S(1)}, u32[]{:S(2)}, u32[]{:S(2)}) collective-permute-start(f32[1024,256]{0,1:T(8,128)S(1)} %add_add_fusion), channel_id=1, source_target_pairs={{0,1},{1,0},{2,3},{3,2},{4,5},{5,4},{6,7},{7,6},{8,9},{9,8},{10,11... | collective-permute-start | bytes 3145736 | tf_op jit(solution)/shard_map/ppermute | solution.py:601
  155.1 4.2 collective-permute-start.5
  176.2 17.2 %copy-start.11 = (bf16[1024,256]{0,1:T(8,128)(2,1)S(1)}, bf16[1024,256]{0,1:T(8,128)(2,1)}, u32[]{:S(2)}) copy-start(bf16[1024,256]{0,1:T(8,128)(2,1)} %copy-done.10) | copy-start | bytes 1572868
  176.2 2.7 collective-permute-start.10
  179.3 14.0 %collective-permute-start.11 = (bf16[1024,256]{0,1:T(8,128)(2,1)S(1)}, bf16[1024,256]{0,1:T(8,128)(2,1)S(1)}, u32[]{:S(2)}, u32[]{:S(2)}) collective-permute-start(bf16[1024,256]{0,1:T(8,128)(2,1)S(1)} %dynamic-slice_convert_fusion.5), channel_id=1, source_target_pairs={{0,1},{1,0},{2,3},{3,2},{4,5},{5,4},{6,7},{7,6},{8,9},{9,8},{10,11... | collective-permute-start | bytes 1572872 | tf_op jit(solution)/shard_map/ppermute | solution.py:601
  193.6 13.4 %copy-start.13 = (bf16[1024,256]{0,1:T(8,128)(2,1)}, bf16[1024,256]{0,1:T(8,128)(2,1)S(1)}, u32[]{:S(2)}) copy-start(bf16[1024,256]{0,1:T(8,128)(2,1)S(1)} %add_convert_fusion.1) | copy-start | bytes 1572868
  193.6 13.5 %copy-start.43 = (bf16[1024,704]{0,1:T(8,128)(2,1)S(1)}, bf16[1024,704]{0,1:T(8,128)(2,1)}, u32[]{:S(2)}) copy-start(bf16[1024,704]{0,1:T(8,128)(2,1)} %get-tuple-element.99) | copy-start | bytes 4325380
  193.6 13.2 %collective-permute-start.12 = (bf16[1024,256]{0,1:T(8,128)(2,1)S(1)}, bf16[1024,256]{0,1:T(8,128)(2,1)S(1)}, u32[]{:S(2)}, u32[]{:S(2)}) collective-permute-start(bf16[1024,256]{0,1:T(8,128)(2,1)S(1)} %add_convert_fusion.1), channel_id=1, source_target_pairs={{0,1},{1,0},{2,3},{3,2},{4,5},{5,4},{6,7},{7,6},{8,9},{9,8},{10,11... | collective-permute-start | bytes 1572872 | tf_op jit(solution)/shard_map/ppermute | solution.py:601
  207.0 8.5 %collective-permute-start.13 = (bf16[1024,512]{0,1:T(8,128)(2,1)S(1)}, bf16[1024,512]{0,1:T(8,128)(2,1)S(1)}, u32[]{:S(2)}, u32[]{:S(2)}) collective-permute-start(bf16[1024,512]{0,1:T(8,128)(2,1)S(1)} %pad_maximum_fusion.11), channel_id=1, source_target_pairs={{0,2},{2,0},{1,3},{3,1},{4,6},{6,4},{5,7},{7,5},{8,10},{10,8},{9,1... | collective-permute-start | bytes 3145736 | tf_op jit(solution)/shard_map/ppermute | solution.py:601
  280.8 2.8 collective-permute-start.6
  284.0 14.3 %collective-permute-start.7 = (bf16[1024,256]{0,1:T(8,128)(2,1)S(1)}, bf16[1024,256]{0,1:T(8,128)(2,1)S(1)}, u32[]{:S(2)}, u32[]{:S(2)}) collective-permute-start(bf16[1024,256]{0,1:T(8,128)(2,1)S(1)} %dynamic-slice_convert_fusion.6), channel_id=1, source_target_pairs={{0,1},{1,0},{2,3},{3,2},{4,5},{5,4},{6,7},{7,6},{8,9},{9,8},{10,11... | collective-permute-start | bytes 1572872 | tf_op jit(solution)/shard_map/ppermute | solution.py:601
  294.9 61.7 %collective-permute-start.14 = (bf16[1024,512]{0,1:T(8,128)(2,1)}, bf16[1024,512]{0,1:T(8,128)(2,1)}, u32[]{:S(2)}, u32[]{:S(2)}) collective-permute-start(bf16[1024,512]{0,1:T(8,128)(2,1)} %dynamic-slice_convert_fusion), channel_id=1, source_target_pairs={{0,2},{2,0},{1,3},{3,1},{4,6},{6,4},{5,7},{7,5},{8,10},{10,8},{9,1... | collective-permute-start | bytes 3145736 | tf_op jit(solution)/shard_map/ppermute | solution.py:601
  359.8 11.0 %collective-permute-start.15 = (bf16[1024,256]{0,1:T(8,128)(2,1)}, bf16[1024,256]{0,1:T(8,128)(2,1)}, u32[]{:S(2)}, u32[]{:S(2)}) collective-permute-start(bf16[1024,256]{0,1:T(8,128)(2,1)} %dynamic-slice_convert_fusion.4), channel_id=1, source_target_pairs={{0,1},{1,0},{2,3},{3,2},{4,5},{5,4},{6,7},{7,6},{8,9},{9,8},{10,11... | collective-permute-start | bytes 1572872 | tf_op jit(solution)/shard_map/ppermute | solution.py:601
  (35 other events, 111.0 us)
Sparse Core Ops, SparseCore 0:
  277.5 279.4 all-reduce.3
